TPU v7x, 512 devices: a whole 4x8x8 slice. The times are simulated.
512 devices in a mesh: il: 64 (over z_hi, y, core), xl: 8 (over z_lo, x).
Axes of the slice: x: 4, y: 8, z: 8 (z_hi: 4, z_lo: 2; z = z_hi * 2 + z_lo), core: 2. Of those that a mesh axis runs over, the one named last changes fastest.
Arguments:
- solution: float32 [256, 512, 512], P('il', 'xl'), may hold values from -6 to 6
- residual: float32 [256, 512, 512], P('il', 'xl'), may hold values from -30 to 30
- direction: float32 [256, 512, 512], P('il', 'xl'), may hold values from -30 to 30
- slope_il: float32 [256, 512, 512], P('il', 'xl'), may hold values from -1.5 to 1.5
- slope_xl: float32 [256, 512, 512], P('il', 'xl'), may hold values from -1.5 to 1.5
- weights: float32 [256, 512, 512], P('il', 'xl'), may hold values from 0.2 to 1
Outputs:
- new_solution: float32 [256, 512, 512], P('il', 'xl')
- new_residual: float32 [256, 512, 512], P('il', 'xl')
- new_direction: float32 [256, 512, 512], P('il', 'xl')
All inputs are finite; a program needn't handle non-finite values.
Results may differ from a plain program's by a relative error of at most 0.00002.
Values sent between devices are 32-bit elements; how exact they have to be, the bound alone decides.
A program may use at most 64 MiB of HBM per device.

v0:
```python
import jax
import jax.numpy as jnp
from jax import lax
from jax.sharding import Mesh
from jax.sharding import PartitionSpec as P

IL = ("il_0", "il_1", "il_2")
XL = ("xl_0", "xl_1")
IL_XL = ("il_0", "il_1", "il_2", "xl_0", "xl_1")
damping = 0.3


def shifted(value, axis, by):
    length = lax.axis_size(axis)
    pairs = [(i, i + by) for i in range(length) if 0 <= i + by < length]
    return lax.ppermute(value, axis, pairs)


def over_axes(value, axes):
    for axis in axes:
        value = lax.psum(value, axis)
    return value


def time_diff(field):
    padded = jnp.pad(field, ((0, 0), (0, 0), (1, 1)))
    return 0.5 * (padded[:, :, 2:] - padded[:, :, :-2])


def normal_apply(direction, slope_il, slope_xl, weights):
    il_rows = direction.shape[0]
    xl_rows = direction.shape[1]
    total_il = il_rows * lax.axis_size(IL)
    total_xl = xl_rows * lax.axis_size(XL)
    start_il = lax.axis_index(IL) * il_rows
    start_xl = lax.axis_index(XL) * xl_rows
    squared = weights * weights
    next_il = shifted(direction[:1], IL, -1)
    next_xl = shifted(direction[:, :1], XL, -1)
    ahead_il = jnp.concatenate([direction[1:], next_il], 0)
    ahead_xl = jnp.concatenate([direction[:, 1:], next_xl], 1)
    slope_t = time_diff(direction)
    keep_il = (start_il + jnp.arange(il_rows) < total_il - 1)[:, None, None]
    keep_xl = (start_xl + jnp.arange(xl_rows) < total_xl - 1)[None, :, None]
    flux_il = jnp.where(keep_il, squared * (ahead_il - direction - slope_il * slope_t), 0.0)
    flux_xl = jnp.where(keep_xl, squared * (ahead_xl - direction - slope_xl * slope_t), 0.0)
    prev_il = shifted(flux_il[-1:], IL, 1)
    prev_xl = shifted(flux_xl[:, -1:], XL, 1)
    behind_il = jnp.concatenate([prev_il, flux_il[:-1]], 0)
    behind_xl = jnp.concatenate([prev_xl, flux_xl[:, :-1]], 1)
    term_il = behind_il - flux_il + time_diff(slope_il * flux_il)
    term_xl = behind_xl - flux_xl + time_diff(slope_xl * flux_xl)
    return term_il + term_xl + damping * direction


def body(solution, residual, direction, slope_il, slope_xl, weights):
    image = normal_apply(direction, slope_il, slope_xl, weights)
    norm_old, along, cross_term, image_norm = (
        over_axes(jnp.sum(residual * residual), IL_XL),
        over_axes(jnp.sum(direction * image), IL_XL),
        over_axes(jnp.sum(residual * image), IL_XL),
        over_axes(jnp.sum(image * image), IL_XL),
    )
    alpha = norm_old / along
    new_residual = residual - alpha * image
    norm_new = norm_old - 2.0 * alpha * cross_term + alpha * alpha * image_norm
    new_solution = solution + alpha * direction
    new_direction = new_residual + norm_new / norm_old * direction
    return (new_solution, new_residual, new_direction)


def solution(mesh):
    torus = Mesh(mesh.devices.reshape(4, 8, 2, 2, 4), ("il_0", "il_1", "il_2", "xl_0", "xl_1"))
    return jax.shard_map(
        body,
        mesh=torus,
        in_specs=(
            P(IL, XL, None),
            P(IL, XL, None),
            P(IL, XL, None),
            P(IL, XL, None),
            P(IL, XL, None),
            P(IL, XL, None),
        ),
        out_specs=(P(IL, XL, None), P(IL, XL, None), P(IL, XL, None)),
        check_vma=False,
    )
```

profile of v0, /device:TPU:8, one launch (start us, length us, event | category | flops | bytes accessed | tf_op | source)
XLA Modules:
  0.0 85.6 jit_solution(10179543610063257132)
XLA Ops:
  0.6 0.8 slice.51
  1.5 0.0 copy-start
  1.5 1.4 %collective-permute-start.2 = (f32[4,1,512]{2,1,0:T(1,128)S(1)}, f32[4,1,512]{2,1,0:T(1,128)S(1)}, u32[]{:S(2)}, u32[]{:S(2)}) collective-permute-start(f32[4,1,512]{2,1,0:T(1,128)S(1)} %slice.51), channel_id=1, source_target_pairs={{1,0},{2,1},{3,2},{4,3},{5,4},{6,5},{7,6},{9,8},{10,9},{11,10},{12... | collective-permute-start | bytes 24584 | tf_op jit(solution)/shard_map/ppermute | solution.py:16
  2.9 0.9 %slice.43 = f32[1,64,512]{2,1,0:T(8,128)S(1)} slice(f32[4,64,512]{2,1,0:T(8,128)} %param.8), slice={[0:1], [0:64], [0:512]} | slice | bytes 262144 | tf_op jit(solution)/shard_map/slice | solution.py:38
  3.8 1.9 %collective-permute-start = (f32[1,64,512]{2,1,0:T(8,128)S(1)}, f32[1,64,512]{2,1,0:T(8,128)S(1)}, u32[]{:S(2)}, u32[]{:S(2)}) collective-permute-start(f32[1,64,512]{2,1,0:T(8,128)S(1)} %slice.43), channel_id=1, source_target_pairs={{8,0},{16,8},{24,16},{32,24},{40,32},{48,40},{56,48},{64,56},{72,6... | collective-permute-start | bytes 393224 | tf_op jit(solution)/shard_map/ppermute | solution.py:16
  5.8 0.0 copy-start.3
  5.8 0.0 copy-done
  5.8 0.0 slice-start
  5.8 0.0 copy-start.2
  5.8 0.1 slice.50
  5.9 1.2 %collective-permute-done.2 = f32[4,1,512]{2,1,0:T(1,128)S(1)} collective-permute-done((f32[4,1,512]{2,1,0:T(1,128)S(1)}, f32[4,1,512]{2,1,0:T(1,128)S(1)}, u32[]{:S(2)}, u32[]{:S(2)}) %collective-permute-start.2) | collective-permute-done | bytes 8224 | tf_op jit(solution)/shard_map/ppermute | solution.py:16
  7.1 1.1 %collective-permute-done = f32[1,64,512]{2,1,0:T(8,128)S(1)} collective-permute-done((f32[1,64,512]{2,1,0:T(8,128)S(1)}, f32[1,64,512]{2,1,0:T(8,128)S(1)}, u32[]{:S(2)}, u32[]{:S(2)}) %collective-permute-start) | collective-permute-done | bytes 131104 | tf_op jit(solution)/shard_map/ppermute | solution.py:16
  8.2 0.0 copy-done.3
  8.2 0.0 slice-done
  8.3 0.0 copy-done.2
  8.3 1.7 %fusion.19 = (f32[4,64,512]{2,1,0:T(8,128)S(1)}, f32[4,64,512]{2,1,0:T(8,128)S(1)}, f32[4,64,512]{2,1,0:T(8,128)S(1)}, f32[4,64,512]{2,1,0:T(8,128)S(1)}) fusion(f32[4,64,512]{2,1,0:T(8,128)S(1)} %copy-done.2, f32[4,64,512]{2,1,0:T(8,128)S(1)} %copy-done, f32[1,64,512]{2,1,0:T(8,128)S(1)} %collective-permute-done, f32[3,64,512]{2,1,0:T(8,128)S(1)} %slice-done, ...), kind=kLoop, calls=%fused_computation.36 | loop fusion | flops 2490368 | bytes 5242948 | tf_op jit(solution)/shard_map/mul | solution.py:51
  10.0 0.0 copy-start.1
  10.0 3.9 %collective-permute-start.1 = (f32[1,64,512]{2,1,0:T(8,128)S(1)}, f32[1,64,512]{2,1,0:T(8,128)S(1)}, u32[]{:S(2)}, u32[]{:S(2)}) collective-permute-start(f32[1,64,512]{2,1,0:T(8,128)S(1)} %slice.56), channel_id=1, source_target_pairs={{0,8},{8,16},{16,24},{24,32},{32,40},{40,48},{48,56},{56,64},{64,7... | collective-permute-start | bytes 393224 | tf_op jit(solution)/shard_map/ppermute | solution.py:16
  13.9 4.5 %collective-permute-start.3 = (f32[4,1,512]{2,1,0:T(1,128)S(1)}, f32[4,1,512]{2,1,0:T(1,128)S(1)}, u32[]{:S(2)}, u32[]{:S(2)}) collective-permute-start(f32[4,1,512]{2,1,0:T(1,128)S(1)} %slice.58), channel_id=1, source_target_pairs={{0,1},{1,2},{2,3},{3,4},{4,5},{5,6},{6,7},{8,9},{9,10},{10,11},{11... | collective-permute-start | bytes 24584 | tf_op jit(solution)/shard_map/ppermute | solution.py:16
  18.5 1.3 %collective-permute-done.3 = f32[4,1,512]{2,1,0:T(1,128)S(1)} collective-permute-done((f32[4,1,512]{2,1,0:T(1,128)S(1)}, f32[4,1,512]{2,1,0:T(1,128)S(1)}, u32[]{:S(2)}, u32[]{:S(2)}) %collective-permute-start.3) | collective-permute-done | bytes 8224 | tf_op jit(solution)/shard_map/ppermute | solution.py:16
  19.8 0.0 collective-permute-done.1
  19.8 0.0 copy-done.1
  19.8 0.0 copy-start.4
  19.8 1.3 %multiply_reduce_fusion = (f32[]{:T(128)}, f32[]{:T(128)}, f32[]{:T(128)}, f32[]{:T(128)}, f32[4,64,512]{2,1,0:T(8,128)S(1)}) fusion(f32[4,64,512]{2,1,0:T(8,128)S(1)} %copy-done.1, f32[4,64,512]{2,1,0:T(8,128)S(1)} %copy-done, f32[4,64,512]{2,1,0:T(8,128)S(1)} %get-tuple-element.34, f32[4,64,512]{2,1,0:T(8,128)S(1)} %get-tuple-element.35, ...), kind=kLoop, calls=%fused_computation.27 | loop fusion | flops 2752508 | bytes 4718608 | tf_op jit(solution)/shard_map/reduce_sum | solution.py:62
  21.1 18.3 %all-reduce.5 = (f32[]{:T(128)}, f32[]{:T(128)}, f32[]{:T(128)}, f32[]{:T(128)}) all-reduce(f32[]{:T(128)} %get-tuple-element.5, f32[]{:T(128)} %get-tuple-element.6, f32[]{:T(128)} %get-tuple-element.4, f32[]{:T(128)} %get-tuple-element.3), channel_id=1, replica_groups=mesh['il_0'=4,'il_1'=8,'il_2'=2,'xl_0'=2,'xl_1'=4] {'il_0'}, use_global_device_ids=true, to_apply=%region_1.2 | all-reduce | flops 4 | bytes 32 | tf_op jit(solution)/shard_map/psum | solution.py:21
  39.4 18.9 %all-reduce.3 = (f32[]{:T(128)}, f32[]{:T(128)}, f32[]{:T(128)}, f32[]{:T(128)}) all-reduce(f32[]{:T(128)} %get-tuple-element.15, f32[]{:T(128)} %get-tuple-element.16, f32[]{:T(128)} %get-tuple-element.17, f32[]{:T(128)} %get-tuple-element.18), channel_id=1, replica_groups=mesh['il_0'=4,'il_1'=8,'il_2'=2,'xl_0'=2,'xl_1'=4] {'il_1'}, use_global_device_ids=true, to_apply=%region_2.3 | all-reduce | flops 4 | bytes 32 | tf_op jit(solution)/shard_map/psum | solution.py:21
  58.3 3.2 %all-reduce.7 = (f32[]{:T(128)}, f32[]{:T(128)}, f32[]{:T(128)}, f32[]{:T(128)}) all-reduce(f32[]{:T(128)} %get-tuple-element.7, f32[]{:T(128)} %get-tuple-element.8, f32[]{:T(128)} %get-tuple-element.9, f32[]{:T(128)} %get-tuple-element.10), channel_id=1, replica_groups=mesh['il_0'=4,'il_1'=8,'il_2'=2,'xl_0'=2,'xl_1'=4] {'il_2'}, use_global_device_ids=true, to_apply=%region_3.4 | all-reduce | flops 4 | bytes 32 | tf_op jit(solution)/shard_map/psum | solution.py:21
  61.5 7.6 %all-reduce.6 = (f32[]{:T(128)}, f32[]{:T(128)}, f32[]{:T(128)}, f32[]{:T(128)}) all-reduce(f32[]{:T(128)} %get-tuple-element.23, f32[]{:T(128)} %get-tuple-element.24, f32[]{:T(128)} %get-tuple-element.25, f32[]{:T(128)} %get-tuple-element.26), channel_id=1, replica_groups=mesh['il_0'=4,'il_1'=8,'il_2'=2,'xl_0'=2,'xl_1'=4] {'xl_0'}, use_global_device_ids=true, to_apply=%region_4.5 | all-reduce | flops 4 | bytes 32 | tf_op jit(solution)/shard_map/psum | solution.py:21
  69.1 11.2 %all-reduce.4 = (f32[]{:T(128)}, f32[]{:T(128)}, f32[]{:T(128)}, f32[]{:T(128)}) all-reduce(f32[]{:T(128)} %get-tuple-element.19, f32[]{:T(128)} %get-tuple-element.20, f32[]{:T(128)} %get-tuple-element.21, f32[]{:T(128)} %get-tuple-element.22), channel_id=1, replica_groups=mesh['il_0'=4,'il_1'=8,'il_2'=2,'xl_0'=2,'xl_1'=4] {'xl_1'}, use_global_device_ids=true, to_apply=%region_5.6 | all-reduce | flops 4 | bytes 32 | tf_op jit(solution)/shard_map/psum | solution.py:21
  84.3 0.0 copy-done.4
  84.3 1.4 %multiply_add_fusion = (f32[4,64,512]{2,1,0:T(8,128)}, f32[4,64,512]{2,1,0:T(8,128)}, f32[4,64,512]{2,1,0:T(8,128)}) fusion(f32[4,64,512]{2,1,0:T(8,128)S(1)} %copy-done, f32[]{:T(128)S(6)} %div.7, f32[4,64,512]{2,1,0:T(8,128)S(1)} %copy-done.1, f32[4,64,512]{2,1,0:T(8,128)S(1)} %get-tuple-element.29, f32[]{:T(128)S(6)} %div.6, f32[4,64,512]{2,1,0:T(8,128)S(1)} %copy-done.4), kind=kLoop, calls=%fused_computation.26 | loop fusion | flops 786432 | bytes 3670024 | tf_op jit(solution)/shard_map/add | solution.py:68
  (5 shorter events, 0.1 us)
Async XLA Ops:
  1.5 4.3 %copy-start = (f32[4,64,512]{2,1,0:T(8,128)S(1)}, f32[4,64,512]{2,1,0:T(8,128)}, u32[]{:S(2)}) copy-start(f32[4,64,512]{2,1,0:T(8,128)} %param.8) | copy-start | bytes 1572868
  1.5 5.7 %collective-permute-start.2 = (f32[4,1,512]{2,1,0:T(1,128)S(1)}, f32[4,1,512]{2,1,0:T(1,128)S(1)}, u32[]{:S(2)}, u32[]{:S(2)}) collective-permute-start(f32[4,1,512]{2,1,0:T(1,128)S(1)} %slice.51), channel_id=1, source_target_pairs={{1,0},{2,1},{3,2},{4,3},{5,4},{6,5},{7,6},{9,8},{10,9},{11,10},{12... | collective-permute-start | bytes 24584 | tf_op jit(solution)/shard_map/ppermute | solution.py:16
  3.8 4.4 %collective-permute-start = (f32[1,64,512]{2,1,0:T(8,128)S(1)}, f32[1,64,512]{2,1,0:T(8,128)S(1)}, u32[]{:S(2)}, u32[]{:S(2)}) collective-permute-start(f32[1,64,512]{2,1,0:T(8,128)S(1)} %slice.43), channel_id=1, source_target_pairs={{8,0},{16,8},{24,16},{32,24},{40,32},{48,40},{56,48},{64,56},{72,6... | collective-permute-start | bytes 393224 | tf_op jit(solution)/shard_map/ppermute | solution.py:16
  5.8 2.5 %copy-start.3 = (f32[4,64,512]{2,1,0:T(8,128)S(1)}, f32[4,64,512]{2,1,0:T(8,128)}, u32[]{:S(2)}) copy-start(f32[4,64,512]{2,1,0:T(8,128)} %param.11) | copy-start | bytes 1572868
  5.8 2.4 %slice-start = ((f32[4,64,512]{2,1,0:T(8,128)}), f32[3,64,512]{2,1,0:T(8,128)S(1)}, s32[]{:S(2)}) async-start(f32[4,64,512]{2,1,0:T(8,128)} %param.8), calls=%async_computation | async-start | bytes 786432 | tf_op jit(solution)/shard_map/slice | solution.py:40
  5.8 2.4 %copy-start.2 = (f32[4,64,512]{2,1,0:T(8,128)S(1)}, f32[4,64,512]{2,1,0:T(8,128)}, u32[]{:S(2)}) copy-start(f32[4,64,512]{2,1,0:T(8,128)} %param.9) | copy-start | bytes 1572868
  10.0 9.8 %copy-start.1 = (f32[4,64,512]{2,1,0:T(8,128)S(1)}, f32[4,64,512]{2,1,0:T(8,128)}, u32[]{:S(2)}) copy-start(f32[4,64,512]{2,1,0:T(8,128)} %param.7) | copy-start | bytes 1572868
  10.0 9.8 %collective-permute-start.1 = (f32[1,64,512]{2,1,0:T(8,128)S(1)}, f32[1,64,512]{2,1,0:T(8,128)S(1)}, u32[]{:S(2)}, u32[]{:S(2)}) collective-permute-start(f32[1,64,512]{2,1,0:T(8,128)S(1)} %slice.56), channel_id=1, source_target_pairs={{0,8},{8,16},{16,24},{24,32},{32,40},{40,48},{48,56},{56,64},{64,7... | collective-permute-start | bytes 393224 | tf_op jit(solution)/shard_map/ppermute | solution.py:16
  13.9 5.9 %collective-permute-start.3 = (f32[4,1,512]{2,1,0:T(1,128)S(1)}, f32[4,1,512]{2,1,0:T(1,128)S(1)}, u32[]{:S(2)}, u32[]{:S(2)}) collective-permute-start(f32[4,1,512]{2,1,0:T(1,128)S(1)} %slice.58), channel_id=1, source_target_pairs={{0,1},{1,2},{2,3},{3,4},{4,5},{5,6},{6,7},{8,9},{9,10},{10,11},{11... | collective-permute-start | bytes 24584 | tf_op jit(solution)/shard_map/ppermute | solution.py:16
  19.8 64.5 %copy-start.4 = (f32[4,64,512]{2,1,0:T(8,128)S(1)}, f32[4,64,512]{2,1,0:T(8,128)}, u32[]{:S(2)}) copy-start(f32[4,64,512]{2,1,0:T(8,128)} %param.6) | copy-start | bytes 1572868
where the time goes:
time: 86.1 us; the launch traced here: 85.6 us
  blocking collectives  59.2 us (69%)
  starting transfers between devices  11.7 us (14%)
  between operations  4.8 us (6%)
  other arithmetic  4.35 us (5%)
  waiting for transfers between devices  3.66 us (4%)
  local copies, waits for them, and re-layouts  1.9 us (2%)
    psum x5, blocking collectives, over_axes(): value = lax.psum(value, axis)  59.2 us
    ppermute x4, starting transfers between devices, shifted(): return lax.ppermute(value, axis, pairs)  11.7 us
    ppermute x4, waiting for transfers between devices, shifted(): return lax.ppermute(value, axis, pairs)  3.66 us
  transfers between devices with their start and end apart: 4, of which 3 were waited for; matrix products, arithmetic and copies ran while one was open for 1% of the time, Pallas kernels for 0%

commit v1 on v0

--- a/solution.py
+++ b/solution.py
@@ -18,7 +18,7 @@
 
 def over_axes(value, axes):
     for axis in axes:
-        value = lax.psum(value, axis)
+        value = jnp.sum(lax.all_gather(value, axis), axis=0)
     return value
 
 

time: 86.1 us -> 132 us (1.53)
  local copies, waits for them, and re-layouts: 1.9 us -> 37.8 us
  other arithmetic: 4.35 us -> 18.7 us
  blocking collectives: 59.2 us -> 54.8 us
  starting transfers between devices: 11.7 us -> 8.65 us
  waiting for transfers between devices: 3.66 us -> 5.69 us
    psum x5 -> x0, blocking collectives: 59.2 us -> none  [over_axes(): value = lax.psum(value, axis)]
    unnamed x0 -> x5, blocking collectives: none -> 54.8 us
    unnamed x10 -> x53, local copies, waits for them, and re-layouts: 0.03 us -> 34.7 us
    reduce_sum x0 -> x20, other arithmetic: none -> 12.3 us  [over_axes(): value = jnp.sum(lax.all_gather(value, axis), axis=0)]
    ppermute x4, starting transfers between devices: 11.7 us -> 8.65 us  [shifted(): return lax.ppermute(value, axis, pairs)]
    ppermute x4, waiting for transfers between devices: 3.66 us -> 5.69 us  [shifted(): return lax.ppermute(value, axis, pairs)]
  transfers between devices with their start and end apart: 4 -> 4, of which waited for: 3 -> 2; matrix products, arithmetic and copies ran while one was open for 1% -> 3% of each run, Pallas kernels for 0% -> 0%
where the time goes in v1:
time: 132 us; the launch traced here: 131 us
  blocking collectives  54.8 us (42%)
  local copies, waits for them, and re-layouts  37.8 us (29%)
  other arithmetic  18.7 us (14%)
  starting transfers between devices  8.65 us (7%)
  waiting for transfers between devices  5.69 us (4%)
  between operations  4.83 us (4%)
    unnamed x5, blocking collectives  54.8 us
    unnamed x53, local copies, waits for them, and re-layouts  34.7 us
    reduce_sum x20, other arithmetic, over_axes(): value = jnp.sum(lax.all_gather(value, axis), axis=0)  12.3 us
    ppermute x4, starting transfers between devices, shifted(): return lax.ppermute(value, axis, pairs)  8.65 us
    ppermute x4, waiting for transfers between devices, shifted(): return lax.ppermute(value, axis, pairs)  5.69 us
  transfers between devices with their start and end apart: 4, of which 2 were waited for; matrix products, arithmetic and copies ran while one was open for 3% of the time, Pallas kernels for 0%

profile of v1, /device:TPU:8, one launch (start us, length us, event | category | flops | bytes accessed | tf_op | source)
XLA Modules:
  0.0 130.5 jit_solution(421471415768966524)
XLA Ops:
  0.6 1.0 slice.43
  1.6 1.9 %collective-permute-start = (f32[1,64,512]{2,1,0:T(8,128)S(1)}, f32[1,64,512]{2,1,0:T(8,128)}, u32[]{:S(2)}, u32[]{:S(2)}) collective-permute-start(f32[1,64,512]{2,1,0:T(8,128)S(1)} %slice.43), channel_id=1, source_target_pairs={{8,0},{16,8},{24,16},{32,24},{40,32},{48,40},{56,48},{64,56},{72,6... | collective-permute-start | bytes 393224 | tf_op jit(solution)/shard_map/ppermute | solution.py:16
  3.5 0.8 slice.51
  4.4 1.3 collective-permute-start.2
  5.7 1.2 slice.50
  7.0 3.0 %collective-permute-done.2 = f32[4,1,512]{2,1,0:T(1,128)S(1)} collective-permute-done((f32[4,1,512]{2,1,0:T(1,128)S(1)}, f32[4,1,512]{2,1,0:T(1,128)S(1)}, u32[]{:S(2)}, u32[]{:S(2)}) %collective-permute-start.2) | collective-permute-done | bytes 8224 | tf_op jit(solution)/shard_map/ppermute | solution.py:16
  10.0 1.8 %fusion.19 = (f32[4,64,512]{2,1,0:T(8,128)S(1)}, f32[4,64,512]{2,1,0:T(8,128)S(1)}, f32[4,64,512]{2,1,0:T(8,128)S(1)}, f32[4,64,512]{2,1,0:T(8,128)S(1)}) fusion(f32[4,64,512]{2,1,0:T(8,128)S(1)} %copy-done.2, f32[4,64,512]{2,1,0:T(8,128)S(1)} %copy-done, f32[1,64,512]{2,1,0:T(8,128)} %collective-permute-done, f32[3,64,512]{2,1,0:T(8,128)S(1)} %slice-done, ...), kind=kLoop, calls=%fused_computation.36 | loop fusion | flops 2490368 | bytes 5242948 | tf_op jit(solution)/shard_map/mul | solution.py:51
  11.8 2.1 %collective-permute-start.1 = (f32[1,64,512]{2,1,0:T(8,128)S(1)}, f32[1,64,512]{2,1,0:T(8,128)S(1)}, u32[]{:S(2)}, u32[]{:S(2)}) collective-permute-start(f32[1,64,512]{2,1,0:T(8,128)S(1)} %slice.56), channel_id=1, source_target_pairs={{0,8},{8,16},{16,24},{24,32},{32,40},{40,48},{48,56},{56,64},{64,7... | collective-permute-start | bytes 393224 | tf_op jit(solution)/shard_map/ppermute | solution.py:16
  13.8 3.4 %collective-permute-start.3 = (f32[4,1,512]{2,1,0:T(1,128)S(1)}, f32[4,1,512]{2,1,0:T(1,128)S(1)}, u32[]{:S(2)}, u32[]{:S(2)}) collective-permute-start(f32[4,1,512]{2,1,0:T(1,128)S(1)} %slice.58), channel_id=1, source_target_pairs={{0,1},{1,2},{2,3},{3,4},{4,5},{5,6},{6,7},{8,9},{9,10},{10,11},{11... | collective-permute-start | bytes 24584 | tf_op jit(solution)/shard_map/ppermute | solution.py:16
  17.2 1.3 %dynamic-slice = u32[1]{0:T(128)} dynamic-slice(u32[512]{0:T(512)} %constant.56, u32[]{:T(128)S(6)} %add.70), dynamic_slice_sizes={1} | dynamic-slice | bytes 12
  18.6 2.7 %collective-permute-done.1 = f32[1,64,512]{2,1,0:T(8,128)S(1)} collective-permute-done((f32[1,64,512]{2,1,0:T(8,128)S(1)}, f32[1,64,512]{2,1,0:T(8,128)S(1)}, u32[]{:S(2)}, u32[]{:S(2)}) %collective-permute-start.1) | collective-permute-done | bytes 131104 | tf_op jit(solution)/shard_map/ppermute | solution.py:16
  21.4 2.1 %multiply_reduce_fusion = (f32[]{:T(128)}, f32[]{:T(128)}, f32[]{:T(128)}, f32[]{:T(128)}, f32[4,64,512]{2,1,0:T(8,128)}) fusion(f32[4,64,512]{2,1,0:T(8,128)S(1)} %copy-done.1, f32[4,64,512]{2,1,0:T(8,128)S(1)} %copy-done, f32[4,64,512]{2,1,0:T(8,128)S(1)} %get-tuple-element.34, f32[4,64,512]{2,1,0:T(8,128)S(1)} %get-tuple-element.35, ...), kind=kLoop, calls=%fused_computation.27 | loop fusion | flops 2752508 | bytes 4718608 | tf_op jit(solution)/shard_map/reduce_sum | solution.py:62
  23.5 1.4 %dynamic-update-slice.10 = f32[4]{0:T(128)S(1)} dynamic-update-slice(f32[4]{0:T(128)S(1)} %broadcast.34.clone.3, f32[1]{0:T(128)} %bitcast.15, u32[]{:T(128)} %bitcast.1) | dynamic-update-slice | bytes 12
  24.9 1.4 %dynamic-update-slice.15 = f32[4]{0:T(128)S(1)} dynamic-update-slice(f32[4]{0:T(128)S(1)} %broadcast.34.clone.4, f32[1]{0:T(128)} %bitcast.20, u32[]{:T(128)} %bitcast.1) | dynamic-update-slice | bytes 12
  26.4 1.4 %dynamic-update-slice.5 = f32[4]{0:T(128)S(1)} dynamic-update-slice(f32[4]{0:T(128)S(1)} %broadcast.34.clone.2, f32[1]{0:T(128)} %bitcast.10, u32[]{:T(128)} %bitcast.1) | dynamic-update-slice | bytes 12
  27.8 1.4 %dynamic-update-slice = f32[4]{0:T(128)S(1)} dynamic-update-slice(f32[4]{0:T(128)S(1)} %broadcast.34.clone.1, f32[1]{0:T(128)} %bitcast, u32[]{:T(128)} %bitcast.1) | dynamic-update-slice | bytes 12
  29.1 1.3 dynamic-slice.1
  30.4 14.9 %all-reduce.25 = (f32[4]{0:T(128)S(1)}, f32[4]{0:T(128)S(1)}, f32[4]{0:T(128)S(1)}, f32[4]{0:T(128)S(1)}) all-reduce(f32[4]{0:T(128)S(1)} %dynamic-update-slice, f32[4]{0:T(128)S(1)} %dynamic-update-slice.5, f32[4]{0:T(128)S(1)} %dynamic-update-slice.10, ...), channel_id=1, replica_groups=mesh['il_0'=4,'il_1'=8,'il_2'=2,'xl_0'=2,'xl_1'=4] {'il_0'}, use_global_device_ids=true, to_apply=%add.3 | all-reduce | flops 16 | bytes 128
  45.3 0.6 reduce_sum.229
  45.9 0.7 reduce_sum.235
  46.6 1.4 %dynamic-update-slice.11 = f32[8]{0:T(128)S(1)} dynamic-update-slice(f32[8]{0:T(128)S(1)} %broadcast.31.clone.2, f32[1]{0:T(128)} %bitcast.16, u32[]{:T(128)} %bitcast.3) | dynamic-update-slice | bytes 12
  48.0 1.4 %dynamic-update-slice.16 = f32[8]{0:T(128)S(1)} dynamic-update-slice(f32[8]{0:T(128)S(1)} %broadcast.31.clone.3, f32[1]{0:T(128)} %bitcast.21, u32[]{:T(128)} %bitcast.3) | dynamic-update-slice | bytes 12
  50.1 1.4 %dynamic-update-slice.6 = f32[8]{0:T(128)S(1)} dynamic-update-slice(f32[8]{0:T(128)S(1)} %broadcast.31.clone.1, f32[1]{0:T(128)} %bitcast.11, u32[]{:T(128)} %bitcast.3) | dynamic-update-slice | bytes 12
  52.1 1.4 %dynamic-update-slice.1 = f32[8]{0:T(128)S(1)} dynamic-update-slice(f32[8]{0:T(128)S(1)} %broadcast.31.clone, f32[1]{0:T(128)} %bitcast.2, u32[]{:T(128)} %bitcast.3) | dynamic-update-slice | bytes 12
  53.5 1.3 dynamic-slice.2
  54.7 20.6 %all-reduce.23 = (f32[8]{0:T(128)S(1)}, f32[8]{0:T(128)S(1)}, f32[8]{0:T(128)S(1)}, f32[8]{0:T(128)S(1)}) all-reduce(f32[8]{0:T(128)S(1)} %dynamic-update-slice.1, f32[8]{0:T(128)S(1)} %dynamic-update-slice.6, f32[8]{0:T(128)S(1)} %dynamic-update-slice.11, ...), channel_id=1, replica_groups=mesh['il_0'=4,'il_1'=8,'il_2'=2,'xl_0'=2,'xl_1'=4] {'il_1'}, use_global_device_ids=true, to_apply=%add.4 | all-reduce | flops 32 | bytes 256
  75.9 0.7 reduce_sum.236
  76.6 1.4 %dynamic-update-slice.12 = f32[2]{0:T(128)S(1)} dynamic-update-slice(f32[2]{0:T(128)S(1)} %broadcast.33.clone.3, f32[1]{0:T(128)} %bitcast.17, u32[]{:T(128)} %bitcast.5) | dynamic-update-slice | bytes 12
  78.0 1.4 %dynamic-update-slice.17 = f32[2]{0:T(128)S(1)} dynamic-update-slice(f32[2]{0:T(128)S(1)} %broadcast.33.clone.4, f32[1]{0:T(128)} %bitcast.22, u32[]{:T(128)} %bitcast.5) | dynamic-update-slice | bytes 12
  80.1 1.4 %dynamic-update-slice.7 = f32[2]{0:T(128)S(1)} dynamic-update-slice(f32[2]{0:T(128)S(1)} %broadcast.33.clone.2, f32[1]{0:T(128)} %bitcast.12, u32[]{:T(128)} %bitcast.5) | dynamic-update-slice | bytes 12
  82.1 1.4 %dynamic-update-slice.2 = f32[2]{0:T(128)S(1)} dynamic-update-slice(f32[2]{0:T(128)S(1)} %broadcast.33.clone.1, f32[1]{0:T(128)} %bitcast.4, u32[]{:T(128)} %bitcast.5) | dynamic-update-slice | bytes 12
  83.5 1.3 dynamic-slice.3
  84.7 2.4 %all-reduce.27 = (f32[2]{0:T(128)S(1)}, f32[2]{0:T(128)S(1)}, f32[2]{0:T(128)S(1)}, f32[2]{0:T(128)S(1)}) all-reduce(f32[2]{0:T(128)S(1)} %dynamic-update-slice.2, f32[2]{0:T(128)S(1)} %dynamic-update-slice.7, f32[2]{0:T(128)S(1)} %dynamic-update-slice.12, ...), channel_id=1, replica_groups=mesh['il_0'=4,'il_1'=8,'il_2'=2,'xl_0'=2,'xl_1'=4] {'il_2'}, use_global_device_ids=true, to_apply=%add.5 | all-reduce | flops 8 | bytes 64
  87.2 0.6 reduce_sum.231
  87.8 0.7 reduce_sum.237
  88.5 1.4 %dynamic-update-slice.13 = f32[2]{0:T(128)S(1)} dynamic-update-slice(f32[2]{0:T(128)S(1)} %broadcast.33.clone.6, f32[1]{0:T(128)} %bitcast.18, u32[]{:T(128)} %bitcast.7) | dynamic-update-slice | bytes 12
  89.9 1.4 %dynamic-update-slice.18 = f32[2]{0:T(128)S(1)} dynamic-update-slice(f32[2]{0:T(128)S(1)} %broadcast.33.clone.7, f32[1]{0:T(128)} %bitcast.23, u32[]{:T(128)} %bitcast.7) | dynamic-update-slice | bytes 12
  91.9 1.4 %dynamic-update-slice.8 = f32[2]{0:T(128)S(1)} dynamic-update-slice(f32[2]{0:T(128)S(1)} %broadcast.33.clone.5, f32[1]{0:T(128)} %bitcast.13, u32[]{:T(128)} %bitcast.7) | dynamic-update-slice | bytes 12
  93.9 1.4 %dynamic-update-slice.3 = f32[2]{0:T(128)S(1)} dynamic-update-slice(f32[2]{0:T(128)S(1)} %broadcast.33.clone, f32[1]{0:T(128)} %bitcast.6, u32[]{:T(128)} %bitcast.7) | dynamic-update-slice | bytes 12
  95.3 1.3 dynamic-slice.4
  96.6 5.5 %all-reduce.26 = (f32[2]{0:T(128)S(1)}, f32[2]{0:T(128)S(1)}, f32[2]{0:T(128)S(1)}, f32[2]{0:T(128)S(1)}) all-reduce(f32[2]{0:T(128)S(1)} %dynamic-update-slice.3, f32[2]{0:T(128)S(1)} %dynamic-update-slice.8, f32[2]{0:T(128)S(1)} %dynamic-update-slice.13, ...), channel_id=1, replica_groups=mesh['il_0'=4,'il_1'=8,'il_2'=2,'xl_0'=2,'xl_1'=4] {'xl_0'}, use_global_device_ids=true, to_apply=%add.6 | all-reduce | flops 8 | bytes 64
  102.7 0.7 reduce_sum.238
  103.4 1.4 %dynamic-update-slice.14 = f32[4]{0:T(128)S(1)} dynamic-update-slice(f32[4]{0:T(128)S(1)} %broadcast.34.clone.6, f32[1]{0:T(128)} %bitcast.19, u32[]{:T(128)} %bitcast.9) | dynamic-update-slice | bytes 12
  104.8 1.4 %dynamic-update-slice.19 = f32[4]{0:T(128)S(1)} dynamic-update-slice(f32[4]{0:T(128)S(1)} %broadcast.34.clone.7, f32[1]{0:T(128)} %bitcast.24, u32[]{:T(128)} %bitcast.9) | dynamic-update-slice | bytes 12
  106.8 1.4 %dynamic-update-slice.9 = f32[4]{0:T(128)S(1)} dynamic-update-slice(f32[4]{0:T(128)S(1)} %broadcast.34.clone.5, f32[1]{0:T(128)} %bitcast.14, u32[]{:T(128)} %bitcast.9) | dynamic-update-slice | bytes 12
  108.8 1.4 %dynamic-update-slice.4 = f32[4]{0:T(128)S(1)} dynamic-update-slice(f32[4]{0:T(128)S(1)} %broadcast.34.clone, f32[1]{0:T(128)} %bitcast.8, u32[]{:T(128)} %bitcast.9) | dynamic-update-slice | bytes 12
  110.2 11.4 %all-reduce.24 = (f32[4]{0:T(128)S(1)}, f32[4]{0:T(128)S(1)}, f32[4]{0:T(128)S(1)}, f32[4]{0:T(128)S(1)}) all-reduce(f32[4]{0:T(128)S(1)} %dynamic-update-slice.4, f32[4]{0:T(128)S(1)} %dynamic-update-slice.9, f32[4]{0:T(128)S(1)} %dynamic-update-slice.14, ...), channel_id=1, replica_groups=mesh['il_0'=4,'il_1'=8,'il_2'=2,'xl_0'=2,'xl_1'=4] {'xl_1'}, use_global_device_ids=true, to_apply=%add.7 | all-reduce | flops 16 | bytes 128
  128.0 2.5 %multiply_add_fusion = (f32[4,64,512]{2,1,0:T(8,128)}, f32[4,64,512]{2,1,0:T(8,128)}, f32[4,64,512]{2,1,0:T(8,128)}) fusion(f32[4,64,512]{2,1,0:T(8,128)S(1)} %copy-done, f32[]{:T(128)S(6)} %div.7, f32[4,64,512]{2,1,0:T(8,128)S(1)} %copy-done.1, f32[4,64,512]{2,1,0:T(8,128)} %get-tuple-element.29, f32[]{:T(128)S(6)} %div.6, f32[4,64,512]{2,1,0:T(8,128)} %param.6), kind=kLoop, calls=%fused_computation.26 | loop fusion | flops 786432 | bytes 3670024 | tf_op jit(solution)/shard_map/add | solution.py:68
  (51 shorter events, 8.5 us)
Async XLA Ops:
  0.6 9.3 %copy-start.3 = (f32[4,64,512]{2,1,0:T(8,128)S(1)}, f32[4,64,512]{2,1,0:T(8,128)}, u32[]{:S(2)}) copy-start(f32[4,64,512]{2,1,0:T(8,128)} %param.11) | copy-start | bytes 1572868
  1.6 8.3 %collective-permute-start = (f32[1,64,512]{2,1,0:T(8,128)S(1)}, f32[1,64,512]{2,1,0:T(8,128)}, u32[]{:S(2)}, u32[]{:S(2)}) collective-permute-start(f32[1,64,512]{2,1,0:T(8,128)S(1)} %slice.43), channel_id=1, source_target_pairs={{8,0},{16,8},{24,16},{32,24},{40,32},{48,40},{56,48},{64,56},{72,6... | collective-permute-start | bytes 393224 | tf_op jit(solution)/shard_map/ppermute | solution.py:16
  4.4 5.5 %collective-permute-start.2 = (f32[4,1,512]{2,1,0:T(1,128)S(1)}, f32[4,1,512]{2,1,0:T(1,128)S(1)}, u32[]{:S(2)}, u32[]{:S(2)}) collective-permute-start(f32[4,1,512]{2,1,0:T(1,128)S(1)} %slice.51), channel_id=1, source_target_pairs={{1,0},{2,1},{3,2},{4,3},{5,4},{6,5},{7,6},{9,8},{10,9},{11,10},{12... | collective-permute-start | bytes 24584 | tf_op jit(solution)/shard_map/ppermute | solution.py:16
  5.7 4.2 %copy-start = (f32[4,64,512]{2,1,0:T(8,128)S(1)}, f32[4,64,512]{2,1,0:T(8,128)}, u32[]{:S(2)}) copy-start(f32[4,64,512]{2,1,0:T(8,128)} %param.8) | copy-start | bytes 1572868
  5.7 4.2 %copy-start.2 = (f32[4,64,512]{2,1,0:T(8,128)S(1)}, f32[4,64,512]{2,1,0:T(8,128)}, u32[]{:S(2)}) copy-start(f32[4,64,512]{2,1,0:T(8,128)} %param.9) | copy-start | bytes 1572868
  6.9 3.0 %slice-start = ((f32[4,64,512]{2,1,0:T(8,128)}), f32[3,64,512]{2,1,0:T(8,128)S(1)}, s32[]{:S(2)}) async-start(f32[4,64,512]{2,1,0:T(8,128)} %param.8), calls=%async_computation | async-start | bytes 786432 | tf_op jit(solution)/shard_map/slice | solution.py:40
  11.7 9.6 %copy-start.1 = (f32[4,64,512]{2,1,0:T(8,128)S(1)}, f32[4,64,512]{2,1,0:T(8,128)}, u32[]{:S(2)}) copy-start(f32[4,64,512]{2,1,0:T(8,128)} %param.7) | copy-start | bytes 1572868
  11.8 9.6 %collective-permute-start.1 = (f32[1,64,512]{2,1,0:T(8,128)S(1)}, f32[1,64,512]{2,1,0:T(8,128)S(1)}, u32[]{:S(2)}, u32[]{:S(2)}) collective-permute-start(f32[1,64,512]{2,1,0:T(8,128)S(1)} %slice.56), channel_id=1, source_target_pairs={{0,8},{8,16},{16,24},{24,32},{32,40},{40,48},{48,56},{56,64},{64,7... | collective-permute-start | bytes 393224 | tf_op jit(solution)/shard_map/ppermute | solution.py:16
  13.8 4.8 %collective-permute-start.3 = (f32[4,1,512]{2,1,0:T(1,128)S(1)}, f32[4,1,512]{2,1,0:T(1,128)S(1)}, u32[]{:S(2)}, u32[]{:S(2)}) collective-permute-start(f32[4,1,512]{2,1,0:T(1,128)S(1)} %slice.58), channel_id=1, source_target_pairs={{0,1},{1,2},{2,3},{3,4},{4,5},{5,6},{6,7},{8,9},{9,10},{10,11},{11... | collective-permute-start | bytes 24584 | tf_op jit(solution)/shard_map/ppermute | solution.py:16
